TPU v7x, 32 devices: a whole 2x2x4 slice. The times are simulated.
32 devices in a mesh: dp: 2 (over x), expert: 16 (over z, y, core).
Axes of the slice: x: 2, y: 2, z: 4, core: 2. Of those that a mesh axis runs over, the one named last changes fastest.
Arguments:
- tokens: bfloat16 [256, 4096], P('dp', 'expert'), may hold values from -6 to 6
- norm_gain: float32 [4096], replicated, may hold values from 0.1 to 1.9
- routes: int32 [256, 2], P('dp'), may hold values from 0 to 15, all different within a row; in each aligned block of 128 rows (0 to 127, 128 to 255, ...) at most 20 rows name the same one
- route_prob: float32 [256, 2], P('dp'), may hold values from 0.2 to 1
- gate_weight: bfloat16 [16, 4096, 256], P('expert', None, 'dp'), may hold values from -0.09375 to 0.09375
- up_weight: bfloat16 [16, 4096, 256], P('expert', None, 'dp'), may hold values from -0.09375 to 0.09375
- down_weight: bfloat16 [16, 256, 4096], P('expert', 'dp'), may hold values from -0.375 to 0.375
- key_value_weight: bfloat16 [4096, 2048], P('expert'), may hold values from -0.09375 to 0.09375
- key_value_target: bfloat16 [256, 2048], P('dp', 'expert'), may hold values from -6 to 6
- concept_mask: int32 [256], P('dp'), may hold values 0 or 1
Outputs:
- down_grad: bfloat16 [16, 256, 4096], P('expert', 'dp')
- key_value_grad: float32 [4096, 2048], P('expert', 'dp')
Inputs may be any that keep to these rules, and one draw needn't show every extreme that they name: `routes`: in each aligned block of 128 rows no expert is named by more than 20 rows; the two choices of a token differ.
All inputs are finite; a program needn't handle non-finite values. No bound on the sum of `concept_mask` on one device may be relied on, other than what follows from the above.
Results may differ from a plain program's by a relative error of at most 0.033.
Values may be sent and summed in bfloat16 or wider, within the bound.
A program may use at most 64 MiB of HBM per device.

v0:
```python
import jax
import jax.numpy as jnp
from jax import lax
from jax.sharding import PartitionSpec as P

eps_norm = 1e-06


def slot_targets(routes, expert_count, capacity):
    flat = routes.reshape(-1)
    onehot = (flat[:, None] == jnp.arange(expert_count, dtype=jnp.int32)[None, :]).astype(jnp.int32)
    before = jnp.cumsum(onehot, axis=0) - onehot
    return flat * capacity + jnp.sum(before * onehot, axis=1)


def per_device(
    tokens,
    norm_gain,
    routes,
    route_prob,
    gate_weight,
    up_weight,
    down_weight,
    key_value_weight,
    key_value_target,
    concept_mask,
):
    token_rows, width = tokens.shape
    top_count = routes.shape[1]
    expert_count = lax.axis_size("expert")
    capacity = 5 * token_rows * top_count // (4 * expert_count)
    model_width = width * expert_count
    position = slot_targets(routes, expert_count, capacity)
    prob_flat = route_prob.reshape(-1)

    def place_rows(pair_rows):
        filled = (
            jnp.zeros((expert_count * capacity, width), jnp.bfloat16).at[position].set(pair_rows)
        )
        return filled.reshape(expert_count, capacity, width)

    values = tokens.astype(jnp.float32)
    total_sq = lax.psum(jnp.sum(values * values, axis=1), "expert")
    scale = lax.rsqrt(total_sq / model_width + eps_norm)
    local_gain = lax.dynamic_slice_in_dim(norm_gain, lax.axis_index("expert") * width, width)
    outgoing = (values * scale[:, None] * local_gain[None, :]).astype(jnp.bfloat16)
    send_slots = place_rows(jnp.repeat(outgoing, top_count, axis=0))
    arrived = lax.all_to_all(send_slots, "expert", split_axis=0, concat_axis=2, tiled=True)[0]
    rows = lax.all_gather(arrived, "dp", axis=0, tiled=True)
    gate_val = jnp.dot(rows, gate_weight[0], preferred_element_type=jnp.float32)
    up_val = jnp.dot(rows, up_weight[0], preferred_element_type=jnp.float32)
    hidden = (jax.nn.silu(gate_val) * up_val).astype(jnp.bfloat16)
    expert_out = lax.psum_scatter(
        jnp.dot(hidden, down_weight[0], preferred_element_type=jnp.float32).astype(jnp.bfloat16),
        "dp",
        scatter_dimension=0,
        tiled=True,
    )
    returned = lax.all_to_all(expert_out[None], "expert", split_axis=2, concat_axis=0, tiled=True)
    picked = returned.reshape(expert_count * capacity, width)[position].astype(jnp.float32)
    expert_mix = (picked * prob_flat[:, None]).reshape(token_rows, top_count, width).sum(axis=1)
    state = (tokens.astype(jnp.float32) + expert_mix).astype(jnp.bfloat16)
    proj_term = jnp.dot(state, key_value_weight, preferred_element_type=jnp.float32)
    proj_cols = lax.psum_scatter(
        proj_term.astype(jnp.bfloat16), "expert", scatter_dimension=1, tiled=True
    ).astype(jnp.float32)
    mask_col = concept_mask.astype(jnp.float32)[:, None]
    cotangent_cols = (
        mask_col * (proj_cols - key_value_target.astype(jnp.float32)) * token_rows ** (-0.5)
    ).astype(jnp.bfloat16)
    cotangent = lax.all_gather(cotangent_cols, "expert", axis=1, tiled=True)
    grad_term = jnp.einsum("tw,tk->wk", state, cotangent, preferred_element_type=jnp.float32)
    key_value_grad = lax.psum_scatter(
        grad_term.astype(jnp.bfloat16), "dp", scatter_dimension=1, tiled=True
    ).astype(jnp.float32)
    state_grad = jnp.einsum(
        "tk,wk->tw", cotangent, key_value_weight, preferred_element_type=jnp.float32
    )
    pair_grad = (jnp.repeat(state_grad, top_count, axis=0) * prob_flat[:, None]).astype(
        jnp.bfloat16
    )
    grad_slots = place_rows(pair_grad)
    landed = lax.all_to_all(grad_slots, "expert", split_axis=0, concat_axis=2, tiled=True)[0]
    down_total = jnp.einsum(
        "rf,rd->fd",
        hidden,
        lax.all_gather(landed, "dp", axis=0, tiled=True),
        preferred_element_type=jnp.float32,
    )
    return (down_total.astype(jnp.bfloat16)[None], key_value_grad)


def solution(mesh):
    placed = (
        P("dp", "expert"),
        P(),
        P("dp", None),
        P("dp", None),
        P("expert", None, "dp"),
        P("expert", None, "dp"),
        P("expert", "dp", None),
        P("expert", None),
        P("dp", "expert"),
        P("dp"),
    )
    return jax.shard_map(
        per_device,
        mesh=mesh,
        in_specs=placed,
        out_specs=(P("expert", "dp", None), P("expert", "dp")),
        check_vma=False,
    )
```

profile of v0, /device:TPU:0, one launch (start us, length us, event | category | flops | bytes accessed | tf_op | source)
XLA Modules:
  0.0 244.3 jit_solution(14645099253849093850)
XLA Ops:
  7.2 0.9 copy.34
  8.1 0.1 eq.29
  8.3 0.1 eq.25
  8.4 0.7 broadcast_multiply_fusion
  9.1 0.6 reduce-window.6
  9.7 0.2 slice_reduce_fusion
  10.0 0.1 mul.83
  10.2 0.9 fusion.7
  11.1 34.9 %psum.7 = f32[128]{0:T(128)S(1)} all-reduce(f32[128]{0:T(128)S(1)} %fusion.7), channel_id=1, replica_groups=mesh['dp'=2,'expert'=16] {'expert'}, use_global_device_ids=true, to_apply=%region_4.5 | all-reduce | flops 128 | bytes 1024 | tf_op jit(solution)/shard_map/psum | solution.py:43
  46.1 0.8 dynamic_slice.3
  46.8 0.9 fusion.9
  48.0 1.5 scatter_custom_fusion
  49.5 11.6 %all_to_all.45 = bf16[16,20,256]{2,1,0:T(8,128)(2,1)S(1)} all-to-all(bf16[16,20,256]{2,1,0:T(8,128)(2,1)S(1)} %reshape.83), channel_id=1, replica_groups=mesh['dp'=2,'expert'=16] {'expert'}, dimensions={0} | all-to-all | bytes 327680 | tf_op jit(solution)/shard_map/all_to_all | solution.py:48
  61.3 6.8 %all-gather = bf16[2,20,4096]{2,1,0:T(8,128)(2,1)S(1)} all-gather(bf16[1,20,4096]{2,1,0:T(8,128)(2,1)S(1)} %reshape.112), channel_id=1, replica_groups=mesh['dp'=2,'expert'=16] {'dp'}, dimensions={0}, use_global_device_ids=true | all-gather | bytes 491520 | tf_op jit(solution)/shard_map/all_gather | solution.py:49
  68.2 0.3 fusion.5
  68.5 1.5 fusion.2
  70.1 0.3 convolution_convert_fusion.1
  70.4 8.9 %fusion = bf16[24,4096]{1,0:T(8,128)(2,1)S(1)} fusion(bf16[40,4096]{1,0:T(8,128)(2,1)S(1)} %convolution_convert_fusion.1), kind=kCustom, calls=%all-reduce-scatter | all-reduce-scatter fusion | flops 196609 | bytes 524800
  79.3 2.4 collective-permute-start
  81.7 0.6 dynamic-slice.4
  83.0 0.3 collective-permute-done
  83.3 0.4 concatenate
  83.8 2.9 %copy.38 = bf16[1,20,4096]{1,0,2:T(2,128)(2,1)S(1)} copy(bf16[1,20,4096]{2,1,0:T(8,128)(2,1)S(1)} %dynamic-slice_bitcast_fusion) | data formatting | bytes 327680 | tf_op jit(solution)/shard_map/broadcast_in_dim | solution.py:59
  86.6 0.5 broadcast.74
  87.2 23.4 %reduce.2 = bf16[4096,20]{1,0:T(8,128)(2,1)} reduce(bf16[4096,1,20]{2,1,0:T(2,128)(2,1)S(1)} %bitcast.70, bf16[]{:T(256)} %broadcast.74), dimensions={1}, to_apply=%bitcast.58.reduce_sub_computation | reduce | bytes 327682
  110.6 3.9 %reshape.126 = bf16[16,2,2560]{2,1,0:T(2,128)(2,1)} reshape(bf16[4096,20]{1,0:T(8,128)(2,1)} %reduce.2) | data formatting | bytes 327680
  114.5 3.6 %all-to-all-start.1 = ((bf16[16,2,2560]{2,1,0:T(2,128)(2,1)}), bf16[16,2,2560]{2,1,0:T(2,128)(2,1)S(1)}, u32[]{:S(2)}, u32[]{:S(2)}) async-start(bf16[16,2,2560]{2,1,0:T(2,128)(2,1)} %reshape.126), calls=%async_computation.1 | async-start | bytes 327680 | tf_op jit(solution)/shard_map/all_to_all | solution.py:59
  118.1 0.1 copy.41
  118.2 8.3 %all-to-all-done.1 = bf16[16,2,2560]{2,1,0:T(2,128)(2,1)S(1)} async-done(((bf16[16,2,2560]{2,1,0:T(2,128)(2,1)}), bf16[16,2,2560]{2,1,0:T(2,128)(2,1)S(1)}, u32[]{:S(2)}, u32[]{:S(2)}) %all-to-all-start.1) | async-done | bytes 163872 | tf_op jit(solution)/shard_map/all_to_all | solution.py:59
  126.5 2.9 %reshape.127 = bf16[4096,1,20]{2,1,0:T(2,128)(2,1)S(1)} reshape(bf16[16,2,2560]{2,1,0:T(2,128)(2,1)S(1)} %all-to-all-done.1) | data formatting | bytes 327680
  129.4 2.3 copy.39
  131.8 1.2 gather_fusion
  133.0 0.1 reshape.87
  133.2 0.4 multiply_reduce_fusion
  133.6 0.3 convolution_convert_fusion.3
  133.9 1.0 copy.44
  135.0 54.4 %reduce-scatter.9.cloned.1.call-done = bf16[128,128]{1,0:T(8,128)(2,1)} async-done(((bf16[2048,128]{1,0:T(8,128)(2,1)}), bf16[128,128]{1,0:T(8,128)(2,1)}) %reduce-scatter.9.cloned.1.call-update) | async-done | bytes 32784
  189.4 0.9 copy.45
  190.4 20.9 %all_gather.10 = bf16[128,2048]{1,0:T(8,128)(2,1)S(1)} all-gather(bf16[128,128]{1,0:T(8,128)(2,1)S(1)} %multiply_convert_fusion.2), channel_id=1, replica_groups=mesh['dp'=2,'expert'=16] {'expert'}, dimensions={1}, use_global_device_ids=true | all-gather | bytes 557056 | tf_op jit(solution)/shard_map/all_gather | solution.py:71
  211.2 1.4 convolution_convert_fusion.2
  212.7 0.1 mul.99
  212.8 0.5 fusion.22
  213.4 0.2 reshape.85
  213.6 1.6 scatter_custom_fusion.1
  215.3 11.6 %all_to_all.46 = bf16[16,20,256]{2,1,0:T(8,128)(2,1)S(1)} all-to-all(bf16[16,20,256]{2,1,0:T(8,128)(2,1)S(1)} %reshape.86), channel_id=1, replica_groups=mesh['dp'=2,'expert'=16] {'expert'}, dimensions={0} | all-to-all | bytes 327680 | tf_op jit(solution)/shard_map/all_to_all | solution.py:83
  227.0 6.8 %all-gather.1 = bf16[2,20,4096]{2,1,0:T(8,128)(2,1)S(1)} all-gather(bf16[1,20,4096]{2,1,0:T(8,128)(2,1)S(1)} %reshape.114), channel_id=1, replica_groups=mesh['dp'=2,'expert'=16] {'dp'}, dimensions={0}, use_global_device_ids=true | all-gather | bytes 491520 | tf_op jit(solution)/shard_map/all_gather | solution.py:87
  233.9 1.4 fusion.1
  235.3 2.1 convert_element_type.74
  (48 shorter events, 1.5 us)
Async XLA Ops:
  7.2 126.4 %copy-start = (bf16[256,2048]{1,0:T(8,128)(2,1)S(1)}, bf16[256,2048]{1,0:T(8,128)(2,1)}, u32[]{:S(2)}) copy-start(bf16[256,2048]{1,0:T(8,128)(2,1)} %param.17) | copy-start | bytes 3145732
  7.2 61.0 %copy-start.2 = (bf16[1,4096,128]{2,1,0:T(8,128)(2,1)S(1)}, bf16[1,4096,128]{2,1,0:T(8,128)(2,1)}, u32[]{:S(2)}) copy-start(bf16[1,4096,128]{2,1,0:T(8,128)(2,1)} %param.14) | copy-start | bytes 3145732
  68.2 1.9 copy-start.3
  68.2 13.5 %copy-start.6 = (u32[32]{0:T(128)S(1)}, u32[32]{0:T(128)}, u32[]{:S(2)}) copy-start(u32[32]{0:T(128)} %constant.38) | copy-start | bytes 388
  79.3 4.0 %collective-permute-start = (bf16[4,4096]{1,0:T(4,128)(2,1)S(1)}, bf16[4,4096]{1,0:T(4,128)(2,1)S(1)}, u32[]{:S(2)}, u32[]{:S(2)}) collective-permute-start(bf16[4,4096]{1,0:T(4,128)(2,1)S(1)} %slice.11), channel_id=1, source_target_pairs={{0,16},{1,17},{2,18},{3,19},{4,20},{5,21},{6,22},{7,23},{8,24},{9,... | collective-permute-start | bytes 98312
  87.2 31.0 %copy-start.5 = (f32[128,2]{0,1:T(2,128)S(1)}, f32[128,2]{0,1:T(2,128)}, u32[]{:S(2)}) copy-start(f32[128,2]{0,1:T(2,128)} %param.13) | copy-start | bytes 3076
  114.5 12.0 %all-to-all-start.1 = ((bf16[16,2,2560]{2,1,0:T(2,128)(2,1)}), bf16[16,2,2560]{2,1,0:T(2,128)(2,1)S(1)}, u32[]{:S(2)}, u32[]{:S(2)}) async-start(bf16[16,2,2560]{2,1,0:T(2,128)(2,1)} %reshape.126), calls=%async_computation.1 | async-start | bytes 327680 | tf_op jit(solution)/shard_map/all_to_all | solution.py:59
  118.1 71.3 %reduce-scatter.9.cloned.1.call-start = ((), (), s32[]{:S(2)}) async-start(), calls=%async_computation.6 | async-start | bytes 557056
  131.7 1.9 copy-start.1
  133.0 2.0 copy-start.7
  133.0 57.3 %copy-start.4 = (bf16[128,128]{1,0:T(8,128)(2,1)S(1)}, bf16[128,128]{1,0:T(8,128)(2,1)}, u32[]{:S(2)}) copy-start(bf16[128,128]{1,0:T(8,128)(2,1)} %param.18) | copy-start | bytes 98308
  134.9 100.4 %reduce-scatter.7.cloned.1.call-start = ((), (), s32[]{:S(2)}) async-start(), calls=%async_computation.5 | async-start | bytes 1572864 | tf_op jit(solution)/shard_map/reduce_scatter | solution.py:73
Sparse Core Ops, SparseCore 0:
  135.0 54.3 reduce-scatter.8
  212.8 17.5 reduce-scatter.6
where the time goes:
time: 245 us; the launch traced here: 244 us
  blocking collectives  101 us (41%)
  waiting for transfers between devices  63.1 us (26%)
  other arithmetic  30.9 us (13%)
  local copies, waits for them, and re-layouts  21.9 us (9%)
  between operations  15.1 us (6%)
  starting transfers between devices  6.08 us (2%)
  matrix products  5.77 us (2%)
    unnamed x4, waiting for transfers between devices  54.8 us
    psum x1, blocking collectives, per_device(): total_sq = lax.psum(jnp.sum(values * values, axis=1), 'expert')  34.9 us
    unnamed x1, other arithmetic  23.4 us
    all_gather x1, blocking collectives, per_device(): cotangent = lax.all_gather(cotangent_cols, 'expert', axis=1, tiled=True)  20.9 us
    unnamed x31, local copies, waits for them, and re-layouts  11.7 us
    all_to_all x1, blocking collectives, per_device(): lax.all_to_all(send_slots, 'expert', split_axis=0, concat_axis=2, tiled=T...  11.6 us
    all_to_all x1, blocking collectives, per_device(): lax.all_to_all(grad_slots, 'expert', split_axis=0, concat_axis=2, tiled=T...  11.6 us
    unnamed x1, blocking collectives  8.89 us
  transfers between devices with their start and end apart: 4, of which 3 were waited for; matrix products, arithmetic and copies ran while one was open for 2% of the time, Pallas kernels for 0%

commit v1 on v0

v1 whole, which is shorter than its diff:
```python
import functools

import jax
import jax.numpy as jnp
from jax import lax
from jax.experimental import pallas as pl
from jax.experimental.pallas import tpu as pltpu
from jax.sharding import PartitionSpec as P

eps_norm = 1e-06
f32, bf16 = jnp.float32, jnp.bfloat16


def dot(a, b, contract):
    return lax.dot_general(a, b, ((contract[:1], contract[1:]), ((), ())), preferred_element_type=f32)


def kernel(
    dp_count,
    expert_count,
    capacity,
    tokens_ref,
    gain_ref,
    routes_ref,
    routes_row_ref,
    prob_ref,
    prob_row_ref,
    mask_ref,
    target_ref,
    gate_hbm,
    up_hbm,
    down_hbm,
    kvw_hbm,
    down_grad_ref,
    kv_grad_ref,
    gate,
    up,
    down,
    kvw,
    kvw_t,
    place,
    rows_out,
    rows_in,
    hidden_ref,
    part_out,
    part_in,
    proj_out,
    proj_in,
    cot,
    cot_swap,
    state_t,
    grad_out,
    grad_in,
    load_sem,
    send_sem,
    recv_sem,
):
    device_count = dp_count * expert_count
    slots, width = rows_out.shape[1:]
    token_rows = tokens_ref.shape[0]
    model_width = width * expert_count
    me_dp, me_expert = lax.axis_index("dp"), lax.axis_index("expert")
    me = me_dp * expert_count + me_expert

    loads = [
        pltpu.make_async_copy(src, dst, load_sem.at[i])
        for i, (src, dst) in enumerate([(kvw_hbm, kvw), (gate_hbm, gate), (up_hbm, up), (down_hbm, down)])
    ]
    for load in loads:
        load.start()

    def place_of(number):
        return lax.div(number, expert_count), lax.rem(number, expert_count)

    barrier = pltpu.get_barrier_semaphore()

    def greet(step, carry):
        pl.semaphore_signal(
            barrier,
            inc=1,
            device_id=place_of(lax.rem(me + step, device_count)),
            device_id_type=pl.DeviceIdType.MESH,
        )
        return carry

    lax.fori_loop(1, device_count, greet, 0)

    def remote(src, dst, phase, target):
        return pltpu.make_async_remote_copy(
            src_ref=src,
            dst_ref=dst,
            send_sem=send_sem.at[phase],
            recv_sem=recv_sem.at[phase],
            device_id=target,
            device_id_type=pl.DeviceIdType.MESH,
        )

    def to_all(phase, source, landing):
        def step_to(step, carry):
            other = lax.rem(me + step, device_count)
            remote(source(other), landing.at[me], phase, place_of(other)).start()
            return carry

        lax.fori_loop(1, device_count, step_to, 0)

    def to_expert(phase, source, landing):
        def step_to(step, carry):
            other = lax.rem(me_expert + step, expert_count)
            remote(source(other), landing.at[me_expert], phase, (me_dp, other)).start()
            return carry

        lax.fori_loop(1, expert_count, step_to, 0)

    def to_dp(phase, source, landing):
        def step_to(step, carry):
            other = lax.rem(me_dp + step, dp_count)
            remote(source(other), landing.at[me_dp], phase, (other, me_expert)).start()
            return carry

        lax.fori_loop(1, dp_count, step_to, 0)

    def arrived(phase, landing):
        most = landing.at[pl.ds(0, landing.shape[0] - 1)]
        pltpu.make_async_copy(most, most, recv_sem.at[phase]).wait()

    def sent(phase, landing):
        most = landing.at[pl.ds(0, landing.shape[0] - 1)]
        pltpu.make_async_copy(most, most, send_sem.at[phase]).wait()

    slot_count = expert_count * slots
    older = lax.broadcasted_iota(jnp.int32, (token_rows, token_rows), 0)
    newer = lax.broadcasted_iota(jnp.int32, (token_rows, token_rows), 1)
    before = (older < newer).astype(f32).astype(bf16)
    after = (older > newer).astype(f32).astype(bf16)

    names_row = lax.broadcasted_iota(jnp.int32, (expert_count, token_rows), 0)
    picks_row = [(names_row == routes_row_ref[k : k + 1, :]).astype(f32) for k in range(2)]
    counts_row = dot((picks_row[0] + picks_row[1]).astype(bf16), before, (1, 0))
    number_row = lax.broadcasted_iota(jnp.int32, (slot_count, token_rows), 0)
    total = None
    for k in range(2):
        slot = jnp.sum(picks_row[k] * counts_row, axis=0, keepdims=True).astype(jnp.int32)
        chosen = (number_row == routes_row_ref[k : k + 1, :] * slots + slot).astype(f32)
        place[k] = chosen.astype(bf16)
        total = chosen if total is None else total + chosen
    rows_out[...] = (
        dot(total.astype(bf16), tokens_ref[...], (1, 0)).astype(bf16).reshape(expert_count, slots, width)
    )
    pl.semaphore_wait(barrier, device_count - 1)
    to_all(0, lambda other: rows_out.at[lax.rem(other, expert_count)], rows_in)
    rows_in[me] = rows_out[me_expert]

    loads[0].wait()
    kvw_t[...] = kvw[...].T
    names = lax.broadcasted_iota(jnp.int32, (token_rows, expert_count), 1)
    picks = [(names == routes_ref[:, k : k + 1]).astype(f32) for k in range(2)]
    counts = dot(after, (picks[0] + picks[1]).astype(bf16), (1, 0))
    number = lax.broadcasted_iota(jnp.int32, (token_rows, slot_count), 1)
    gather = []
    for k in range(2):
        slot = jnp.sum(picks[k] * counts, axis=1, keepdims=True).astype(jnp.int32)
        gather.append((number == routes_ref[:, k : k + 1] * slots + slot).astype(f32).astype(bf16))
    for load in loads[1:]:
        load.wait()
    arrived(0, rows_in)

    all_rows = dp_count * slots
    squares = jnp.zeros((all_rows, 1), f32)

    def features(ref, block):
        pieces = [ref[b * expert_count + block] for b in range(dp_count)]
        return jnp.concatenate(pieces, axis=0)

    for f in range(expert_count):
        piece = features(rows_in, f).astype(f32)
        squares = squares + jnp.sum(piece * piece, axis=1, keepdims=True)
    scale = lax.rsqrt(squares / model_width + eps_norm)
    gate_val = jnp.zeros((all_rows, gate.shape[1]), f32)
    up_val = jnp.zeros((all_rows, gate.shape[1]), f32)
    for f in range(expert_count):
        span = pl.ds(f * width, width)
        normed = (features(rows_in, f).astype(f32) * scale * gain_ref[:, span]).astype(bf16)
        gate_val = gate_val + dot(normed, gate[span, :], (1, 0))
        up_val = up_val + dot(normed, up[span, :], (1, 0))
    hidden = (gate_val / (1.0 + jnp.exp(-gate_val)) * up_val).astype(bf16)
    hidden_ref[...] = hidden
    for f in range(expert_count):
        piece = dot(hidden, down[:, pl.ds(f * width, width)], (1, 0)).astype(bf16)
        for b in range(dp_count):
            part_out[b * expert_count + f] = piece[b * slots : (b + 1) * slots]
    to_all(1, lambda other: part_out.at[other], part_in)
    part_in[me] = part_out[me]
    arrived(1, part_in)

    expert_out = part_in[pl.ds(0, expert_count)].astype(f32)
    for b in range(1, dp_count):
        expert_out = expert_out + part_in[pl.ds(b * expert_count, expert_count)].astype(f32)
    expert_out = expert_out.astype(bf16).reshape(slot_count, width)
    state = tokens_ref[...].astype(f32)
    for k in range(2):
        state = state + prob_ref[:, k : k + 1] * dot(gather[k], expert_out, (1, 0))
    state = state.astype(bf16)

    proj = dot(kvw_t[...], state, (1, 1)).astype(bf16)
    proj_out[...] = proj.reshape(proj_out.shape)
    to_expert(2, lambda other: proj_out.at[other], proj_in)
    proj_in[me_expert] = proj_out[me_expert]
    state_t[me_dp] = state.astype(f32).T.astype(bf16)
    to_dp(3, lambda other: state_t.at[me_dp], state_t)
    arrived(2, proj_in)
    key_value = jnp.sum(proj_in[...].astype(f32), axis=0)
    cot[me_expert] = (
        mask_ref[...].astype(f32) * (key_value - target_ref[...].astype(f32)) * token_rows ** (-0.5)
    ).astype(bf16)
    to_expert(4, lambda other: cot.at[me_expert], cot)
    arrived(4, cot)

    share = expert_count // dp_count
    to_dp(5, lambda other: cot.at[pl.ds(other * share, share)], cot_swap)
    cot_swap[me_dp] = cot[pl.ds(me_dp * share, share)]
    cot_all = cot[...].reshape(kvw.shape[1], token_rows)
    state_grad_t = dot(kvw[...], cot_all, (1, 0))
    grads = jnp.zeros((slot_count, width), f32)
    for k in range(2):
        pair_grad = (state_grad_t * prob_row_ref[k : k + 1, :]).astype(bf16)
        grads = grads + dot(place[k], pair_grad, (1, 1))
    grad_out[...] = grads.astype(bf16).reshape(expert_count, slots, width)
    to_all(6, lambda other: grad_out.at[lax.rem(other, expert_count)], grad_in)
    grad_in[me] = grad_out[me_expert]

    arrived(3, state_t)
    arrived(5, cot_swap)
    columns = kv_grad_ref.shape[1]
    kv_grad = jnp.zeros(kv_grad_ref.shape, f32)
    for b in range(dp_count):
        kv_grad = kv_grad + dot(state_t[b], cot_swap[b].reshape(columns, token_rows), (1, 1))
    kv_grad_ref[...] = kv_grad
    hidden_t = hidden_ref[...].astype(f32).T.astype(bf16)
    arrived(6, grad_in)
    for f in range(expert_count):
        down_grad_ref[:, pl.ds(f * width, width)] = dot(hidden_t, features(grad_in, f), (1, 0)).astype(bf16)

    for phase, landing in enumerate([rows_in, part_in, proj_in, state_t, cot, cot_swap, grad_in]):
        sent(phase, landing)


def per_device(
    tokens,
    norm_gain,
    routes,
    route_prob,
    gate_weight,
    up_weight,
    down_weight,
    key_value_weight,
    key_value_target,
    concept_mask,
):
    token_rows, width = tokens.shape
    dp_count, expert_count = lax.axis_size("dp"), lax.axis_size("expert")
    device_count = dp_count * expert_count
    capacity = 5 * token_rows * routes.shape[1] // (4 * expert_count)
    slots = -(-capacity // 16) * 16
    slot_count = expert_count * slots
    model_width, units = gate_weight.shape[1:]
    keys = key_value_weight.shape[1]
    own_keys = keys // expert_count
    in_vmem = pl.BlockSpec(memory_space=pltpu.VMEM)
    in_any = pl.BlockSpec(memory_space=pl.ANY)
    pieces = pltpu.VMEM((device_count, slots, width), bf16)
    own_pieces = pltpu.VMEM((expert_count, slots, width), bf16)
    key_pieces = pltpu.VMEM((expert_count, own_keys, token_rows), bf16)
    down_grad, kv_grad = pl.pallas_call(
        functools.partial(kernel, dp_count, expert_count, capacity),
        out_shape=(
            jax.ShapeDtypeStruct((units, model_width), bf16),
            jax.ShapeDtypeStruct((width, keys // dp_count), f32),
        ),
        in_specs=[in_vmem] * 8 + [in_any] * 4,
        out_specs=(in_vmem, in_vmem),
        scratch_shapes=[
            pltpu.VMEM((model_width, units), bf16),
            pltpu.VMEM((model_width, units), bf16),
            pltpu.VMEM((units, model_width), bf16),
            pltpu.VMEM((width, keys), bf16),
            pltpu.VMEM((keys, width), bf16),
            pltpu.VMEM((2, slot_count, token_rows), bf16),
            own_pieces,
            pieces,
            pltpu.VMEM((dp_count * slots, units), bf16),
            pieces,
            pieces,
            key_pieces,
            key_pieces,
            key_pieces,
            pltpu.VMEM((dp_count, expert_count // dp_count, own_keys, token_rows), bf16),
            pltpu.VMEM((dp_count, width, token_rows), bf16),
            own_pieces,
            pieces,
            pltpu.SemaphoreType.DMA((4,)),
            pltpu.SemaphoreType.DMA((7,)),
            pltpu.SemaphoreType.DMA((7,)),
        ],
        compiler_params=pltpu.CompilerParams(
            collective_id=0, has_side_effects=True, vmem_limit_bytes=48 * 1024 * 1024
        ),
    )(
        tokens,
        norm_gain[None, :],
        routes,
        routes.T,
        route_prob,
        route_prob.T,
        concept_mask[None, :],
        key_value_target.T,
        gate_weight[0],
        up_weight[0],
        down_weight[0],
        key_value_weight,
    )
    return (down_grad[None], kv_grad)


def solution(mesh):
    placed = (
        P("dp", "expert"),
        P(),
        P("dp", None),
        P("dp", None),
        P("expert", None, "dp"),
        P("expert", None, "dp"),
        P("expert", "dp", None),
        P("expert", None),
        P("dp", "expert"),
        P("dp"),
    )
    return jax.shard_map(
        per_device,
        mesh=mesh,
        in_specs=placed,
        out_specs=(P("expert", "dp", None), P("expert", "dp")),
        check_vma=False,
    )
```

time: 245 us -> 81.6 us (0.33)
  blocking collectives: 101 us -> 0 us
  Pallas kernels: 0 us -> 71.6 us
  waiting for transfers between devices: 63.1 us -> 0 us
  other arithmetic: 30.9 us -> 0 us
  between operations: 15.1 us -> 0.66 us
  local copies, waits for them, and re-layouts: 21.9 us -> 8.56 us
  starting transfers between devices: 6.08 us -> 0 us
  matrix products: 5.77 us -> 0 us
    pallas_call x0 -> x1, Pallas kernels: none -> 71.6 us  [per_device(): pl.pallas_call(functools.partial(kernel, dp_count, expert_count, capacity...]
    unnamed x4 -> x0, waiting for transfers between devices: 54.8 us -> none
    psum x1 -> x0, blocking collectives: 34.9 us -> none  [per_device(): total_sq = lax.psum(jnp.sum(values * values, axis=1), 'expert')]
    all_gather x3 -> x0, blocking collectives: 34.5 us -> none  [the longest x1 20.9 us: per_device(): cotangent = lax.all_gather(cotangent_cols, 'expert', axis=1, tiled=True)]
    unnamed x1 -> x0, other arithmetic: 23.4 us -> none
    all_to_all x2 -> x0, blocking collectives: 23.2 us -> none  [the longest x1 11.6 us: per_device(): lax.all_to_all(send_slots, 'expert', split_axis=0, concat_axis=2, tiled=T...]
    unnamed x1 -> x0, blocking collectives: 8.89 us -> none
    all_to_all x1 -> x0, waiting for transfers between devices: 8.28 us -> none  [per_device(): lax.all_to_all(expert_out[None], 'expert', split_axis=2, concat_axis=0, t...]
  transfers between devices with their start and end apart: 4 -> 0, of which waited for: 3 -> 0; matrix products, arithmetic and copies ran while one was open for 2% -> 0% of each run, Pallas kernels for 0% -> 0%
where the time goes in v1:
time: 81.6 us; the launch traced here: 80.9 us
  Pallas kernels  71.6 us (88%)
  local copies, waits for them, and re-layouts  8.56 us (10%)
    pallas_call x1, Pallas kernels, per_device(): pl.pallas_call(functools.partial(kernel, dp_count, expert_count, capacity...  71.6 us
    unnamed x21, local copies, waits for them, and re-layouts  8.56 us

profile of v1, /device:TPU:0, one launch (start us, length us, event | category | flops | bytes accessed | tf_op | source)
XLA Modules:
  0.0 80.9 jit_solution(1118042701681593121)
XLA Ops:
  0.6 0.9 %copy.12 = bf16[128,128]{0,1:T(8,128)(2,1)S(1)} copy(bf16[128,128]{1,0:T(8,128)(2,1)} %param.18) | data formatting | bytes 65536 | tf_op args[8]
  1.5 0.0 copy-start.5
  1.5 0.7 copy-done.5
  2.2 0.0 copy-start.6
  2.2 0.0 copy-start.3
  2.2 0.1 copy.13.routes_ref
  2.3 0.6 copy-done.6
  2.9 0.0 copy-start.4
  2.9 0.0 copy-start.7
  2.9 0.1 copy.14.prob_ref
  3.0 0.1 copy-done.3
  3.0 0.5 copy-done.4
  3.6 0.0 copy-done.7
  3.6 0.0 copy-start
  3.6 1.2 %copy-done = bf16[1,4096,128]{2,1,0:T(8,128)(2,1)S(1)} copy-done((bf16[1,4096,128]{2,1,0:T(8,128)(2,1)S(1)}, bf16[1,4096,128]{2,1,0:T(8,128)(2,1)}, u32[]{:S(2)}) %copy-start) | copy-done | bytes 1048600
  4.8 0.0 copy-start.1
  4.8 1.2 %copy-done.1 = bf16[1,4096,128]{2,1,0:T(8,128)(2,1)S(1)} copy-done((bf16[1,4096,128]{2,1,0:T(8,128)(2,1)S(1)}, bf16[1,4096,128]{2,1,0:T(8,128)(2,1)}, u32[]{:S(2)}) %copy-start.1) | copy-done | bytes 1048600
  6.0 0.0 copy-start.2
  6.0 1.2 %copy-done.2 = bf16[1,128,4096]{2,1,0:T(8,128)(2,1)S(1)} copy-done((bf16[1,128,4096]{2,1,0:T(8,128)(2,1)S(1)}, bf16[1,128,4096]{2,1,0:T(8,128)(2,1)}, u32[]{:S(2)}) %copy-start.2) | copy-done | bytes 1048600
  7.3 71.6 %shard_map.113 = (bf16[128,4096]{1,0:T(8,128)(2,1)S(1)}, f32[256,1024]{1,0:T(8,128)S(1)}) custom-call(bf16[128,256]{1,0:T(8,128)(2,1)S(1)} %copy-done.3, f32[1,4096]{1,0:T(1,128)S(1)} %bitcast.14, s32[128,2]{1,0:T(8,128)S(1)} %copy.13.routes_ref, s32[2,128]{1,0:T(2,128)S(1)} %bitcast.15, f32[128,2]{1,0:T(8,128)S(1)} %copy.14.prob_ref, ...), custom_call_target="tpu_custom_call" | custom-call | tf_op jit(solution)/shard_map/pallas_call | solution.py:273
  78.9 1.0 %copy.17 = bf16[1,128,4096]{2,1,0:T(8,128)(2,1)} copy(bf16[1,128,4096]{2,1,0:T(8,128)(2,1)S(1)} %bitcast.9) | data formatting | bytes 2097152
  79.9 1.0 %copy.18 = f32[256,1024]{1,0:T(8,128)} copy(f32[256,1024]{1,0:T(8,128)S(1)} %get-tuple-element.9) | data formatting | bytes 2097152
Async XLA Ops:
  1.5 0.7 copy-start.5
  2.2 0.7 copy-start.6
  2.2 0.9 %copy-start.3 = (bf16[128,256]{1,0:T(8,128)(2,1)S(1)}, bf16[128,256]{1,0:T(8,128)(2,1)}, u32[]{:S(2)}) copy-start(bf16[128,256]{1,0:T(8,128)(2,1)} %tokens_ref.1) | copy-start | bytes 196612
  2.9 0.7 copy-start.4
  2.9 0.7 copy-start.7
  3.6 1.2 %copy-start = (bf16[1,4096,128]{2,1,0:T(8,128)(2,1)S(1)}, bf16[1,4096,128]{2,1,0:T(8,128)(2,1)}, u32[]{:S(2)}) copy-start(bf16[1,4096,128]{2,1,0:T(8,128)(2,1)} %param.14) | copy-start | bytes 3145732
  4.8 1.2 %copy-start.1 = (bf16[1,4096,128]{2,1,0:T(8,128)(2,1)S(1)}, bf16[1,4096,128]{2,1,0:T(8,128)(2,1)}, u32[]{:S(2)}) copy-start(bf16[1,4096,128]{2,1,0:T(8,128)(2,1)} %param.15) | copy-start | bytes 3145732
  6.0 1.2 %copy-start.2 = (bf16[1,128,4096]{2,1,0:T(8,128)(2,1)S(1)}, bf16[1,128,4096]{2,1,0:T(8,128)(2,1)}, u32[]{:S(2)}) copy-start(bf16[1,128,4096]{2,1,0:T(8,128)(2,1)} %param.16) | copy-start | bytes 3145732

commit v2 on v0

v2 whole, which is shorter than its diff:
```python
import functools

import jax
import jax.numpy as jnp
from jax import lax
from jax.experimental import pallas as pl
from jax.experimental.pallas import tpu as pltpu
from jax.sharding import PartitionSpec as P

eps_norm = 1e-06
f32, bf16 = jnp.float32, jnp.bfloat16


def dot(a, b, contract):
    return lax.dot_general(a, b, ((contract[:1], contract[1:]), ((), ())), preferred_element_type=f32)


def swapped(index, step):
    bit = 1
    while bit <= step:
        if step & bit:
            index = index + bit - 2 * bit * lax.rem(lax.div(index, bit), 2)
        bit *= 2
    return index


def sizes(dp_count, expert_count, token_rows, top_count, width):
    capacity = 5 * token_rows * top_count // (4 * expert_count)
    halves = width // 128
    return capacity, halves, -(-halves * capacity // 16) * 16


def sem_plan(dp_count, groups):
    plan, at = {}, 0
    for name, count in (
        ("rows", groups),
        ("rows_x", dp_count * groups),
        ("part_x", dp_count * groups),
        ("part", 1),
        ("proj_core", 2),
        ("proj_mid", groups),
        ("proj", 1),
        ("state", 1),
        ("cot", groups),
        ("cot_mid", groups),
        ("cot_core", 1),
        ("swap", 1),
        ("swap_core", 1),
        ("grad", groups),
        ("grad_x", dp_count * groups),
    ):
        plan[name] = at
        at += count
    return plan, at


def kernel(
    dp_count,
    expert_count,
    top_count,
    tokens_hbm,
    routes_hbm,
    prob_hbm,
    mask_hbm,
    gain_hbm,
    target_hbm,
    kvw_hbm,
    gate_hbm,
    up_hbm,
    down_hbm,
    down_grad_ref,
    kv_grad_ref,
    tokens_ref,
    routes_ref,
    prob_ref,
    mask_ref,
    gain_ref,
    target_ref,
    kvw,
    gate,
    up,
    down,
    kvw_t,
    place,
    rows_out,
    rows_in,
    hidden_ref,
    part_out,
    part_x,
    part_sum,
    part_in,
    proj_out,
    proj_core,
    mid_out,
    proj_mid,
    last_out,
    proj_in,
    cot,
    cot_swap,
    state_t,
    grad_out,
    grad_in,
    load_sem,
    send_sem,
    recv_sem,
):
    token_rows, width = tokens_ref.shape
    rows = rows_out.shape[1]
    capacity, halves, rows_again = sizes(dp_count, expert_count, token_rows, top_count, width)
    assert rows == rows_again
    units = gate.shape[1]
    model_width = width * expert_count
    groups = expert_count // 4
    recv_at, _ = sem_plan(dp_count, groups)
    send_at = {name: i for i, name in enumerate(recv_at)}
    me_dp, me = lax.axis_index("dp"), lax.axis_index("expert")
    me_group, me_mid, me_low = lax.div(me, 4), lax.rem(lax.div(me, 2), 2), lax.rem(me, 2)
    own_first = me_dp * expert_count

    loads = [
        pltpu.make_async_copy(src, dst, load_sem.at[i])
        for i, (src, dst) in enumerate(
            [
                (tokens_hbm, tokens_ref),
                (routes_hbm, routes_ref),
                (prob_hbm, prob_ref),
                (mask_hbm, mask_ref),
                (gain_hbm, gain_ref),
                (target_hbm, target_ref),
                (kvw_hbm, kvw),
                (gate_hbm, gate),
                (up_hbm, up),
                (down_hbm, down),
            ]
        )
    ]
    for load in loads:
        load.start()

    def expert_at(group, mid, low):
        return group * 4 + mid * 2 + low

    barrier = pltpu.get_barrier_semaphore()
    for step in range(1, expert_count):
        pl.semaphore_signal(
            barrier,
            inc=1,
            device_id=(me_dp, lax.rem(me + step, expert_count)),
            device_id_type=pl.DeviceIdType.MESH,
        )
    for step in range(1, dp_count):
        pl.semaphore_signal(
            barrier,
            inc=1,
            device_id=(lax.rem(me_dp + step, dp_count), me),
            device_id_type=pl.DeviceIdType.MESH,
        )

    def send(name, number, src, dst, target):
        pltpu.make_async_remote_copy(
            src_ref=src,
            dst_ref=dst,
            send_sem=send_sem.at[send_at[name]],
            recv_sem=recv_sem.at[recv_at[name] + number],
            device_id=target,
            device_id_type=pl.DeviceIdType.MESH,
        ).start()

    def arrived(name, number, like):
        pltpu.make_async_copy(like, like, recv_sem.at[recv_at[name] + number]).wait()

    leaving = []

    def leaves(name, like):
        leaving.append((name, like))

    def to_group(name, step, source, landing, numbered):
        group = swapped(me_group, step)
        for turn in range(1 if step == 0 else 0, 4):
            other = group * 4 + lax.rem(lax.rem(me, 4) + turn, 4)
            send(name, step if numbered else 0, source.at[other], landing, (me_dp, other))

    def dispatch(name, source, landing, work):
        name_x = name + "_x"
        for step in reversed(range(groups)):
            to_group(name, step, source, landing.at[own_first + me], True)
        landing[own_first + me] = source[me]

        def forward(step):
            count = 3 if step == 0 else 4
            arrived(name, step, landing.at[pl.ds(0, count)])
            span = pl.ds(own_first + swapped(me_group, step) * 4, 4)
            for turn in range(1, dp_count):
                send(name_x, me_dp * groups + step, landing.at[span], landing.at[span], (lax.rem(me_dp + turn, dp_count), me))

        forward(0)
        for step in range(groups):
            if step + 1 < groups:
                forward(step + 1)
            for turn in range(1, dp_count):
                other = lax.rem(me_dp + turn, dp_count)
                arrived(name_x, other * groups + step, landing.at[pl.ds(0, 4)])
            work(swapped(me_group, step))
        leaves(name, landing.at[pl.ds(0, expert_count - 1)])
        leaves(name_x, landing.at[pl.ds(0, (dp_count - 1) * expert_count)])

    place_count = expert_count * rows
    older = lax.broadcasted_iota(jnp.int32, (token_rows, token_rows), 0)
    newer = lax.broadcasted_iota(jnp.int32, (token_rows, token_rows), 1)
    before = (older < newer).astype(f32).astype(bf16)
    same = older == newer

    loads[0].wait()
    loads[1].wait()
    names = lax.broadcasted_iota(jnp.int32, (expert_count, token_rows), 0)
    picks = [(names == routes_ref[k : k + 1, :]).astype(f32) for k in range(top_count)]
    counts = dot(sum(picks).astype(bf16), before, (1, 0))
    number = lax.broadcasted_iota(jnp.int32, (place_count, token_rows), 0)
    position = []
    for k in range(top_count):
        slot = jnp.sum(picks[k] * counts, axis=0, keepdims=True).astype(jnp.int32)
        position.append(routes_ref[k : k + 1, :] * rows + slot)
    sent_rows = jnp.zeros((place_count, 128), f32)
    for h in range(halves):
        both = jnp.zeros((place_count, token_rows), f32)
        for k in range(top_count):
            chosen = (number == position[k] + h * capacity).astype(f32)
            place[k, h] = chosen.astype(bf16)
            both = both + chosen
        sent_rows = sent_rows + dot(both.astype(bf16), tokens_ref[:, h * 128 : (h + 1) * 128], (1, 0))
    rows_out[...] = sent_rows.astype(bf16).reshape(expert_count, rows, 128)
    pl.semaphore_wait(barrier, expert_count - 1 + dp_count - 1)

    def column(row):
        return jnp.sum(jnp.where(same, row, 0), axis=1, keepdims=True)

    all_rows = dp_count * rows
    squares = [jnp.zeros((all_rows, 1), f32)]
    sums = [[jnp.zeros((all_rows, units), f32) for h in range(halves)] for _ in range(2)]

    for load in loads[2:6]:
        load.wait()

    def up_projections(group):
        if not squares[1:]:
            for load in loads[7:]:
                load.wait()
            squares.append(None)
        for i in range(4):
            f = group * 4 + i
            piece = jnp.concatenate([rows_in[b * expert_count + f] for b in range(dp_count)], axis=0).astype(f32)
            squares[0] = squares[0] + jnp.sum(piece * piece, axis=1, keepdims=True)
            for h in range(halves):
                span = pl.ds(pl.multiple_of(f * width + h * 128, 128), 128)
                gained = (piece * gain_ref[:, span]).astype(bf16)
                sums[0][h] = sums[0][h] + dot(gained, gate[span, :], (1, 0))
                sums[1][h] = sums[1][h] + dot(gained, up[span, :], (1, 0))

    dispatch("rows", rows_out, rows_in, up_projections)

    row_number = lax.broadcasted_iota(jnp.int32, (rows, 1), 0)
    for b in range(dp_count):
        span = slice(b * rows, (b + 1) * rows)

        def folded(terms):
            full = jnp.zeros(terms[0].shape, f32)
            for h, term in enumerate(terms):
                full = full + (pltpu.roll(term, rows - h * capacity, 0) if h else term)
            return jnp.where(row_number < capacity, full, 0.0)

        mean = folded([jnp.broadcast_to(squares[0][span], (rows, units))] * halves) / model_width
        scale = lax.rsqrt(mean + eps_norm)
        gate_val = folded([term[span] for term in sums[0]]) * scale
        up_val = folded([term[span] for term in sums[1]]) * scale
        hidden = gate_val / (1.0 + jnp.exp(-gate_val)) * up_val
        for h in range(halves):
            spread = pltpu.roll(hidden, h * capacity, 0) if h else hidden
            hidden_ref[h, span, :] = spread.astype(bf16)

    for step in reversed(range(groups)):
        group = swapped(me_group, step)
        for i in range(4):
            f = group * 4 + i
            piece = jnp.zeros((all_rows, 128), f32)
            for h in range(halves):
                span = pl.ds(pl.multiple_of(f * width + h * 128, 128), 128)
                piece = piece + dot(hidden_ref[h], down[:, span], (1, 0))
            piece = piece.astype(bf16)
            for b in range(dp_count):
                part_out[b * expert_count + f] = piece[b * rows : (b + 1) * rows]
        for turn in range(1, dp_count):
            other = lax.rem(me_dp + turn, dp_count)
            send(
                "part_x",
                me_dp * groups + step,
                part_out.at[pl.ds(other * expert_count + group * 4, 4)],
                part_x.at[pl.ds(own_first + group * 4, 4)],
                (other, me),
            )

    def column_work():
        gather = []
        for k in range(top_count):
            spot = column(position[k])
            lanes = lax.broadcasted_iota(jnp.int32, (token_rows, place_count), 1)
            gather.append([(lanes == spot + h * capacity).astype(f32).astype(bf16) for h in range(halves)])
        return gather, [column(prob_ref[k : k + 1, :]) for k in range(top_count)]

    gather, prob_column = column_work()
    loads[6].wait()
    own_keys = kvw.shape[1] // expert_count
    turned = kvw[...].T
    for g in range(groups):
        for mid in range(2):
            for low in range(2):
                c = expert_at(g, mid, low)
                kvw_t[low, mid, g] = turned[c * own_keys : (c + 1) * own_keys]
    target = target_ref[...].astype(f32).T

    for step in reversed(range(groups)):
        group = swapped(me_group, step)
        total = part_out[pl.ds(own_first + group * 4, 4)].astype(f32)
        for turn in range(1, dp_count):
            other = lax.rem(me_dp + turn, dp_count)
            arrived("part_x", other * groups + step, part_x.at[pl.ds(0, 4)])
            total = total + part_x[pl.ds(other * expert_count + group * 4, 4)].astype(f32)
        part_sum[pl.ds(group * 4, 4)] = total.astype(bf16)
        to_group("part", step, part_sum, part_in.at[me], False)
    leaves("part_x", part_out.at[pl.ds(0, (dp_count - 1) * expert_count)])
    leaves("part", part_in.at[pl.ds(0, expert_count - 1)])
    part_in[me] = part_sum[me]
    arrived("part", 0, part_in.at[pl.ds(0, expert_count - 1)])

    expert_out = part_in[...].reshape(place_count, 128)
    states = []
    for h in range(halves):
        state = tokens_ref[:, h * 128 : (h + 1) * 128].astype(f32)
        for k in range(top_count):
            state = state + prob_column[k] * dot(gather[k][h], expert_out, (1, 0))
        states.append(state)
    state_wide = jnp.concatenate(states, axis=1) if halves > 1 else states[0]
    state = state_wide.astype(bf16)

    def project(low, mid):
        weights = kvw_t[low, mid].reshape(groups * own_keys, width)
        return dot(weights, state, (1, 1)).reshape(groups, own_keys, token_rows)

    sibling = (me_dp, expert_at(me_group, me_mid, 1 - me_low))
    across = (me_dp, expert_at(me_group, 1 - me_mid, me_low))
    for turn, mid in enumerate((1 - me_mid, me_mid)):
        proj_out[turn] = project(1 - me_low, mid).astype(bf16)
        send("proj_core", turn, proj_out.at[turn], proj_core.at[turn], sibling)
    leaves("proj_core", proj_out)
    far, near = project(me_low, 1 - me_mid), project(me_low, me_mid)
    arrived("proj_core", 0, proj_core.at[0])
    mid_out[...] = (far + proj_core[0].astype(f32)).astype(bf16)
    for step in reversed(range(groups)):
        group = swapped(me_group, step)
        send("proj_mid", step, mid_out.at[group], proj_mid.at[group], across)
    leaves("proj_mid", proj_mid)
    arrived("proj_core", 1, proj_core.at[1])
    proj_core[1] = (near + proj_core[1].astype(f32)).astype(bf16)
    state_t[me_dp] = state_wide.T.astype(bf16)
    for turn in range(1, dp_count):
        send("state", 0, state_t.at[me_dp], state_t.at[me_dp], (lax.rem(me_dp + turn, dp_count), me))
    leaves("state", state_t.at[pl.ds(0, dp_count - 1)])
    key_value = None
    for step in reversed(range(groups)):
        group = swapped(me_group, step)
        arrived("proj_mid", step, proj_mid.at[0])
        summed = proj_core[1, group].astype(f32) + proj_mid[group].astype(f32)
        if step:
            last_out[group] = summed.astype(bf16)
            send("proj", 0, last_out.at[group], proj_in.at[me_group], (me_dp, expert_at(group, me_mid, me_low)))
        else:
            proj_in[me_group] = jnp.zeros(proj_in.shape[1:], bf16)
            key_value = summed
    leaves("proj", proj_in.at[pl.ds(0, groups - 1)])
    arrived("proj", 0, proj_in.at[pl.ds(0, groups - 1)])
    key_value = key_value + jnp.sum(proj_in[...].astype(f32), axis=0)
    cot[me] = (mask_ref[...].astype(f32) * (key_value - target) * token_rows ** (-0.5)).astype(bf16)

    for step in reversed(range(1, groups)):
        other = expert_at(swapped(me_group, step), me_mid, me_low)
        send("cot", step, cot.at[me], cot.at[me], (me_dp, other))
    for step in range(groups):
        if step:
            arrived("cot", step, cot.at[0])
        c = expert_at(swapped(me_group, step), me_mid, me_low)
        send("cot_mid", step, cot.at[c], cot.at[c], across)
        send("cot_core", 0, cot.at[c], cot.at[c], sibling)
    for step in range(groups):
        arrived("cot_mid", step, cot.at[0])
        c = expert_at(swapped(me_group, step), 1 - me_mid, me_low)
        send("cot_core", 0, cot.at[c], cot.at[c], sibling)
    leaves("cot", cot.at[pl.ds(0, groups - 1)])
    leaves("cot_mid", cot.at[pl.ds(0, groups)])
    leaves("cot_core", cot.at[pl.ds(0, 2 * groups)])

    share = expert_count // dp_count
    pairs = share // 2
    swap_bytes = cot_swap.at[pl.ds(0, (dp_count - 1) * pairs)]
    for turn in range(1, dp_count):
        other = lax.rem(me_dp + turn, dp_count)
        for i in range(pairs):
            part = 2 * i + me_low
            send("swap", 0, cot.at[other * share + part], cot_swap.at[me_dp * share + part], (other, me))
    leaves("swap", swap_bytes)
    arrived("cot_core", 0, cot.at[pl.ds(0, 2 * groups)])

    state_grad_t = dot(kvw[...], cot[...].reshape(kvw.shape[1], token_rows), (1, 0))
    grads = jnp.zeros((place_count, 128), f32)
    for k in range(top_count):
        pair_grad = (state_grad_t * prob_ref[k : k + 1, :]).astype(bf16)
        for h in range(halves):
            grads = grads + dot(place[k, h], pair_grad[h * 128 : (h + 1) * 128], (1, 1))
    grad_out[...] = grads.astype(bf16).reshape(expert_count, rows, 128)

    hidden_t = [hidden_ref[h].astype(f32).T.astype(bf16) for h in range(halves)]

    def down_gradient(group):
        for i in range(4):
            f = group * 4 + i
            piece = jnp.concatenate([grad_in[b * expert_count + f] for b in range(dp_count)], axis=0)
            for h in range(halves):
                span = pl.ds(pl.multiple_of(f * width + h * 128, 128), 128)
                down_grad_ref[:, span] = dot(hidden_t[h], piece, (1, 0)).astype(bf16)

    dispatch("grad", grad_out, grad_in, down_gradient)

    arrived("swap", 0, swap_bytes)
    for turn in range(1, dp_count):
        other = lax.rem(me_dp + turn, dp_count)
        for i in range(pairs):
            spot = cot_swap.at[other * share + 2 * i + me_low]
            send("swap_core", 0, spot, spot, sibling)
    leaves("swap_core", swap_bytes)
    columns = kv_grad_ref.shape[1]
    kv_grad = dot(state_t[me_dp], cot[pl.ds(me_dp * share, share)].reshape(columns, token_rows), (1, 1))
    arrived("state", 0, state_t.at[pl.ds(0, dp_count - 1)])
    arrived("swap_core", 0, swap_bytes)
    for turn in range(1, dp_count):
        other = lax.rem(me_dp + turn, dp_count)
        theirs = cot_swap[pl.ds(other * share, share)].reshape(columns, token_rows)
        kv_grad = kv_grad + dot(state_t[other], theirs, (1, 1))
    kv_grad_ref[...] = kv_grad

    for name, like in leaving:
        pltpu.make_async_copy(like, like, send_sem.at[send_at[name]]).wait()


def per_device(
    tokens,
    norm_gain,
    routes,
    route_prob,
    gate_weight,
    up_weight,
    down_weight,
    key_value_weight,
    key_value_target,
    concept_mask,
):
    token_rows, width = tokens.shape
    top_count = routes.shape[1]
    dp_count, expert_count = lax.axis_size("dp"), lax.axis_size("expert")
    device_count = dp_count * expert_count
    capacity, halves, rows = sizes(dp_count, expert_count, token_rows, top_count, width)
    groups = expert_count // 4
    model_width, units = gate_weight.shape[1:]
    keys = key_value_weight.shape[1]
    own_keys = keys // expert_count
    in_vmem = pl.BlockSpec(memory_space=pltpu.VMEM)
    in_any = pl.BlockSpec(memory_space=pl.ANY)
    pieces = pltpu.VMEM((device_count, rows, 128), bf16)
    own_pieces = pltpu.VMEM((expert_count, rows, 128), bf16)
    group_keys = pltpu.VMEM((groups, own_keys, token_rows), bf16)
    core_keys = pltpu.VMEM((2, groups, own_keys, token_rows), bf16)
    all_keys = pltpu.VMEM((expert_count, own_keys, token_rows), bf16)
    plan, recv_count = sem_plan(dp_count, groups)
    given = (
        tokens,
        routes.T,
        route_prob.T,
        concept_mask[None, :],
        norm_gain[None, :],
        key_value_target,
        key_value_weight,
        gate_weight[0],
        up_weight[0],
        down_weight[0],
    )
    down_grad, kv_grad = pl.pallas_call(
        functools.partial(kernel, dp_count, expert_count, top_count),
        out_shape=(
            jax.ShapeDtypeStruct((units, model_width), bf16),
            jax.ShapeDtypeStruct((width, keys // dp_count), f32),
        ),
        in_specs=[in_any] * len(given),
        out_specs=(in_vmem, in_vmem),
        scratch_shapes=[pltpu.VMEM(x.shape, x.dtype) for x in given]
        + [
            pltpu.VMEM((2, 2, groups, own_keys, width), bf16),
            pltpu.VMEM((top_count, halves, expert_count * rows, token_rows), bf16),
            own_pieces,
            pieces,
            pltpu.VMEM((halves, dp_count * rows, units), bf16),
            pieces,
            pieces,
            own_pieces,
            own_pieces,
            core_keys,
            core_keys,
            group_keys,
            group_keys,
            group_keys,
            group_keys,
            all_keys,
            all_keys,
            pltpu.VMEM((dp_count, width, token_rows), bf16),
            own_pieces,
            pieces,
            pltpu.SemaphoreType.DMA((len(given),)),
            pltpu.SemaphoreType.DMA((len(plan),)),
            pltpu.SemaphoreType.DMA((recv_count,)),
        ],
        compiler_params=pltpu.CompilerParams(
            collective_id=0, has_side_effects=True, vmem_limit_bytes=62 * 1024 * 1024
        ),
    )(*given)
    return (down_grad[None], kv_grad)


def solution(mesh):
    placed = (
        P("dp", "expert"),
        P(),
        P("dp", None),
        P("dp", None),
        P("expert", None, "dp"),
        P("expert", None, "dp"),
        P("expert", "dp", None),
        P("expert", None),
        P("dp", "expert"),
        P("dp"),
    )
    return jax.shard_map(
        per_device,
        mesh=mesh,
        in_specs=placed,
        out_specs=(P("expert", "dp", None), P("expert", "dp")),
        check_vma=False,
    )
```

time: 245 us -> 64.1 us (0.26)
  blocking collectives: 101 us -> 0 us
  waiting for transfers between devices: 63.1 us -> 0 us
  Pallas kernels: 0 us -> 59.4 us
  other arithmetic: 30.9 us -> 0 us
  local copies, waits for them, and re-layouts: 21.9 us -> 3.35 us
  between operations: 15.1 us -> 0.65 us
  starting transfers between devices: 6.08 us -> 0 us
  matrix products: 5.77 us -> 0 us
    pallas_call x0 -> x1, Pallas kernels: none -> 59.4 us  [per_device(): pl.pallas_call(functools.partial(kernel, dp_count, expert_count, top_coun...]
    unnamed x4 -> x0, waiting for transfers between devices: 54.8 us -> none
    psum x1 -> x0, blocking collectives: 34.9 us -> none  [per_device(): total_sq = lax.psum(jnp.sum(values * values, axis=1), 'expert')]
    all_gather x3 -> x0, blocking collectives: 34.5 us -> none  [the longest x1 20.9 us: per_device(): cotangent = lax.all_gather(cotangent_cols, 'expert', axis=1, tiled=True)]
    unnamed x1 -> x0, other arithmetic: 23.4 us -> none
    all_to_all x2 -> x0, blocking collectives: 23.2 us -> none  [the longest x1 11.6 us: per_device(): lax.all_to_all(send_slots, 'expert', split_axis=0, concat_axis=2, tiled=T...]
    unnamed x1 -> x0, blocking collectives: 8.89 us -> none
    unnamed x31 -> x4, local copies, waits for them, and re-layouts: 11.7 us -> 3.35 us
  transfers between devices with their start and end apart: 4 -> 0, of which waited for: 3 -> 0; matrix products, arithmetic and copies ran while one was open for 2% -> 0% of each run, Pallas kernels for 0% -> 0%
where the time goes in v2:
time: 64.1 us; the launch traced here: 63.4 us
  Pallas kernels  59.4 us (93%)
  local copies, waits for them, and re-layouts  3.35 us (5%)
  between operations  0.65 us (1%)
    pallas_call x1, Pallas kernels, per_device(): pl.pallas_call(functools.partial(kernel, dp_count, expert_count, top_coun...  59.4 us
    unnamed x4, local copies, waits for them, and re-layouts  3.35 us

profile of v2, /device:TPU:0, one launch (start us, length us, event | category | flops | bytes accessed | tf_op | source)
XLA Modules:
  0.0 63.4 jit_solution(5120827509136171647)
XLA Ops:
  0.6 59.4 %shard_map.113 = (bf16[128,4096]{1,0:T(8,128)(2,1)}, f32[256,1024]{1,0:T(8,128)}) custom-call(bf16[128,256]{1,0:T(8,128)(2,1)} %tokens_hbm.1, s32[2,128]{1,0:T(2,128)} %bitcast.13, f32[2,128]{1,0:T(2,128)} %bitcast.14, s32[1,128]{1,0:T(1,128)} %bitcast.15, f32[1,4096]{1,0:T(1,128)} %bitcast.12, bf16[128,128]{1,0:T(8,128)(2,1)} %target_hbm.1, ...), custom_call_target="tpu_custom_call" | custom-call | tf_op jit(solution)/shard_map/pallas_call | solution.py:493
  60.0 0.0 copy-start
  60.1 2.4 %copy.14 = bf16[1,128,4096]{2,1,0:T(8,128)(2,1)} copy(bf16[1,128,4096]{2,1,0:T(8,128)(2,1)} %bitcast.8) | data formatting | bytes 2097152
  62.4 0.0 copy-done
  62.4 1.0 %copy.15 = f32[256,1024]{1,0:T(8,128)} copy(f32[256,1024]{1,0:T(8,128)S(1)} %copy-done) | data formatting | bytes 2097152
Async XLA Ops:
  60.0 2.4 %copy-start = (f32[256,1024]{1,0:T(8,128)S(1)}, f32[256,1024]{1,0:T(8,128)}, u32[]{:S(2)}) copy-start(f32[256,1024]{1,0:T(8,128)} %get-tuple-element.9) | copy-start | bytes 3145732

commit v3 on v2

--- a/solution.py
+++ b/solution.py
@@ -180,7 +180,7 @@
             other = group * 4 + lax.rem(lax.rem(me, 4) + turn, 4)
             send(name, step if numbered else 0, source.at[other], landing, (me_dp, other))
 
-    def dispatch(name, source, landing, work):
+    def dispatch(name, source, landing, work, beside):
         name_x = name + "_x"
         for step in reversed(range(groups)):
             to_group(name, step, source, landing.at[own_first + me], True)
@@ -194,9 +194,11 @@
                 send(name_x, me_dp * groups + step, landing.at[span], landing.at[span], (lax.rem(me_dp + turn, dp_count), me))
 
         forward(0)
+        beside(0)
         for step in range(groups):
             if step + 1 < groups:
                 forward(step + 1)
+                beside(step + 1)
             for turn in range(1, dp_count):
                 other = lax.rem(me_dp + turn, dp_count)
                 arrived(name_x, other * groups + step, landing.at[pl.ds(0, 4)])
@@ -220,14 +222,17 @@
     for k in range(top_count):
         slot = jnp.sum(picks[k] * counts, axis=0, keepdims=True).astype(jnp.int32)
         position.append(routes_ref[k : k + 1, :] * rows + slot)
-    sent_rows = jnp.zeros((place_count, 128), f32)
+    placed, parts = [], []
     for h in range(halves):
         both = jnp.zeros((place_count, token_rows), f32)
         for k in range(top_count):
+            at = (h * top_count + k) * token_rows
             chosen = (number == position[k] + h * capacity).astype(f32)
-            place[k, h] = chosen.astype(bf16)
+            place[:, at : at + token_rows] = chosen.astype(bf16)
             both = both + chosen
-        sent_rows = sent_rows + dot(both.astype(bf16), tokens_ref[:, h * 128 : (h + 1) * 128], (1, 0))
+        placed.append(both.astype(bf16))
+        parts.append(tokens_ref[:, h * 128 : (h + 1) * 128])
+    sent_rows = dot(jnp.concatenate(placed, axis=1), jnp.concatenate(parts, axis=0), (1, 0))
     rows_out[...] = sent_rows.astype(bf16).reshape(expert_count, rows, 128)
     pl.semaphore_wait(barrier, expert_count - 1 + dp_count - 1)
 
@@ -236,7 +241,9 @@
 
     all_rows = dp_count * rows
     squares = [jnp.zeros((all_rows, 1), f32)]
-    sums = [[jnp.zeros((all_rows, units), f32) for h in range(halves)] for _ in range(2)]
+    sums = [jnp.zeros((all_rows, 2 * units), f32)]
+    block_row = lax.rem(lax.broadcasted_iota(jnp.int32, (all_rows, 1), 0), rows)
+    in_half = [(block_row >= h * capacity) & (block_row < (h + 1) * capacity) for h in range(halves)]
 
     for load in loads[2:6]:
         load.wait()
@@ -246,46 +253,46 @@
             for load in loads[7:]:
                 load.wait()
             squares.append(None)
+        sides, weights = [], []
         for i in range(4):
             f = group * 4 + i
             piece = jnp.concatenate([rows_in[b * expert_count + f] for b in range(dp_count)], axis=0).astype(f32)
             squares[0] = squares[0] + jnp.sum(piece * piece, axis=1, keepdims=True)
             for h in range(halves):
                 span = pl.ds(pl.multiple_of(f * width + h * 128, 128), 128)
-                gained = (piece * gain_ref[:, span]).astype(bf16)
-                sums[0][h] = sums[0][h] + dot(gained, gate[span, :], (1, 0))
-                sums[1][h] = sums[1][h] + dot(gained, up[span, :], (1, 0))
-
-    dispatch("rows", rows_out, rows_in, up_projections)
+                sides.append(jnp.where(in_half[h], piece * gain_ref[:, span], 0.0).astype(bf16))
+            span = pl.ds(pl.multiple_of(f * width, 128), width)
+            weights.append(jnp.concatenate([gate[span, :], up[span, :]], axis=1))
+        sums[0] = sums[0] + dot(jnp.concatenate(sides, axis=1), jnp.concatenate(weights, axis=0), (1, 0))
+
+    dispatch("rows", rows_out, rows_in, up_projections, lambda step: None)
 
     row_number = lax.broadcasted_iota(jnp.int32, (rows, 1), 0)
     for b in range(dp_count):
         span = slice(b * rows, (b + 1) * rows)
 
-        def folded(terms):
-            full = jnp.zeros(terms[0].shape, f32)
-            for h, term in enumerate(terms):
-                full = full + (pltpu.roll(term, rows - h * capacity, 0) if h else term)
+        def folded(term):
+            full = term
+            for h in range(1, halves):
+                full = full + pltpu.roll(term, rows - h * capacity, 0)
             return jnp.where(row_number < capacity, full, 0.0)
 
-        mean = folded([jnp.broadcast_to(squares[0][span], (rows, units))] * halves) / model_width
+        mean = folded(jnp.broadcast_to(squares[0][span], (rows, units))) / model_width
         scale = lax.rsqrt(mean + eps_norm)
-        gate_val = folded([term[span] for term in sums[0]]) * scale
-        up_val = folded([term[span] for term in sums[1]]) * scale
+        gate_val = folded(sums[0][span, :units]) * scale
+        up_val = folded(sums[0][span, units:]) * scale
         hidden = gate_val / (1.0 + jnp.exp(-gate_val)) * up_val
         for h in range(halves):
             spread = pltpu.roll(hidden, h * capacity, 0) if h else hidden
-            hidden_ref[h, span, :] = spread.astype(bf16)
+            hidden_ref[span, h * units : (h + 1) * units] = spread.astype(bf16)
 
     for step in reversed(range(groups)):
         group = swapped(me_group, step)
         for i in range(4):
             f = group * 4 + i
-            piece = jnp.zeros((all_rows, 128), f32)
-            for h in range(halves):
-                span = pl.ds(pl.multiple_of(f * width + h * 128, 128), 128)
-                piece = piece + dot(hidden_ref[h], down[:, span], (1, 0))
-            piece = piece.astype(bf16)
+            spans = [pl.ds(pl.multiple_of(f * width + h * 128, 128), 128) for h in range(halves)]
+            weights = jnp.concatenate([down[:, span] for span in spans], axis=0)
+            piece = dot(hidden_ref[...], weights, (1, 0)).astype(bf16)
             for b in range(dp_count):
                 part_out[b * expert_count + f] = piece[b * rows : (b + 1) * rows]
         for turn in range(1, dp_count):
@@ -307,6 +314,7 @@
         return gather, [column(prob_ref[k : k + 1, :]) for k in range(top_count)]
 
     gather, prob_column = column_work()
+    hidden_t = hidden_ref[...].astype(f32).T.astype(bf16)
     loads[6].wait()
     own_keys = kvw.shape[1] // expert_count
     turned = kvw[...].T
@@ -409,41 +417,45 @@
     arrived("cot_core", 0, cot.at[pl.ds(0, 2 * groups)])
 
     state_grad_t = dot(kvw[...], cot[...].reshape(kvw.shape[1], token_rows), (1, 0))
-    grads = jnp.zeros((place_count, 128), f32)
-    for k in range(top_count):
-        pair_grad = (state_grad_t * prob_ref[k : k + 1, :]).astype(bf16)
-        for h in range(halves):
-            grads = grads + dot(place[k, h], pair_grad[h * 128 : (h + 1) * 128], (1, 1))
+    pair_grads = [(state_grad_t * prob_ref[k : k + 1, :]).astype(bf16) for k in range(top_count)]
+    sides = [pair_grads[k][h * 128 : (h + 1) * 128] for h in range(halves) for k in range(top_count)]
+    grads = dot(place[...], jnp.concatenate(sides, axis=1), (1, 1))
     grad_out[...] = grads.astype(bf16).reshape(expert_count, rows, 128)
 
-    hidden_t = [hidden_ref[h].astype(f32).T.astype(bf16) for h in range(halves)]
+    columns = kv_grad_ref.shape[1]
+
+    def beside_grads(step):
+        if step == 0:
+            own = cot[pl.ds(me_dp * share, share)].reshape(columns, token_rows)
+            kv_grad_ref[...] = dot(state_t[me_dp], own, (1, 1))
+        if step == 1:
+            arrived("swap", 0, swap_bytes)
+            for turn in range(1, dp_count):
+                other = lax.rem(me_dp + turn, dp_count)
+                for i in range(pairs):
+                    spot = cot_swap.at[other * share + 2 * i + me_low]
+                    send("swap_core", 0, spot, spot, sibling)
+            leaves("swap_core", swap_bytes)
+        if step == groups - 1:
+            arrived("state", 0, state_t.at[pl.ds(0, dp_count - 1)])
+            arrived("swap_core", 0, swap_bytes)
+            for turn in range(1, dp_count):
+                other = lax.rem(me_dp + turn, dp_count)
+                theirs = cot_swap[pl.ds(other * share, share)].reshape(columns, token_rows)
+                kv_grad_ref[...] += dot(state_t[other], theirs, (1, 1))
 
     def down_gradient(group):
+        pieces = []
         for i in range(4):
             f = group * 4 + i
-            piece = jnp.concatenate([grad_in[b * expert_count + f] for b in range(dp_count)], axis=0)
+            pieces.append(jnp.concatenate([grad_in[b * expert_count + f] for b in range(dp_count)], axis=0))
+        wide = dot(hidden_t, jnp.concatenate(pieces, axis=1), (1, 0)).astype(bf16)
+        for i in range(4):
             for h in range(halves):
-                span = pl.ds(pl.multiple_of(f * width + h * 128, 128), 128)
-                down_grad_ref[:, span] = dot(hidden_t[h], piece, (1, 0)).astype(bf16)
-
-    dispatch("grad", grad_out, grad_in, down_gradient)
-
-    arrived("swap", 0, swap_bytes)
-    for turn in range(1, dp_count):
-        other = lax.rem(me_dp + turn, dp_count)
-        for i in range(pairs):
-            spot = cot_swap.at[other * share + 2 * i + me_low]
-            send("swap_core", 0, spot, spot, sibling)
-    leaves("swap_core", swap_bytes)
-    columns = kv_grad_ref.shape[1]
-    kv_grad = dot(state_t[me_dp], cot[pl.ds(me_dp * share, share)].reshape(columns, token_rows), (1, 1))
-    arrived("state", 0, state_t.at[pl.ds(0, dp_count - 1)])
-    arrived("swap_core", 0, swap_bytes)
-    for turn in range(1, dp_count):
-        other = lax.rem(me_dp + turn, dp_count)
-        theirs = cot_swap[pl.ds(other * share, share)].reshape(columns, token_rows)
-        kv_grad = kv_grad + dot(state_t[other], theirs, (1, 1))
-    kv_grad_ref[...] = kv_grad
+                span = pl.ds(pl.multiple_of((group * 4 + i) * width + h * 128, 128), 128)
+                down_grad_ref[:, span] = wide[h * units : (h + 1) * units, i * 128 : (i + 1) * 128]
+
+    dispatch("grad", grad_out, grad_in, down_gradient, beside_grads)
 
     for name, like in leaving:
         pltpu.make_async_copy(like, like, send_sem.at[send_at[name]]).wait()
@@ -501,10 +513,10 @@
         scratch_shapes=[pltpu.VMEM(x.shape, x.dtype) for x in given]
         + [
             pltpu.VMEM((2, 2, groups, own_keys, width), bf16),
-            pltpu.VMEM((top_count, halves, expert_count * rows, token_rows), bf16),
+            pltpu.VMEM((expert_count * rows, halves * top_count * token_rows), bf16),
             own_pieces,
             pieces,
-            pltpu.VMEM((halves, dp_count * rows, units), bf16),
+            pltpu.VMEM((dp_count * rows, halves * units), bf16),
             pieces,
             pieces,
             own_pieces,
@@ -525,7 +537,7 @@
             pltpu.SemaphoreType.DMA((recv_count,)),
         ],
         compiler_params=pltpu.CompilerParams(
-            collective_id=0, has_side_effects=True, vmem_limit_bytes=62 * 1024 * 1024
+            collective_id=0, has_side_effects=True, vmem_limit_bytes=61 * 1024 * 1024 + 256 * 1024
         ),
     )(*given)
     return (down_grad[None], kv_grad)

time: 64.1 us -> 62.7 us (0.978)
  Pallas kernels: 59.4 us -> 58.6 us
    pallas_call x1, Pallas kernels: 59.4 us -> 58.6 us  [per_device(): pl.pallas_call(functools.partial(kernel, dp_count, expert_count, top_coun...]
where the time goes in v3:
time: 62.7 us; the launch traced here: 62.6 us
  Pallas kernels  58.6 us (93%)
  local copies, waits for them, and re-layouts  3.35 us (5%)
  between operations  0.65 us (1%)
    pallas_call x1, Pallas kernels, per_device(): pl.pallas_call(functools.partial(kernel, dp_count, expert_count, top_coun...  58.6 us
    unnamed x4, local copies, waits for them, and re-layouts  3.35 us

profile of v3, /device:TPU:0, one launch (start us, length us, event | category | flops | bytes accessed | tf_op | source)
XLA Modules:
  0.0 62.6 jit_solution(6850496080246670378)
XLA Ops:
  0.6 58.6 %shard_map.113 = (bf16[128,4096]{1,0:T(8,128)(2,1)}, f32[256,1024]{1,0:T(8,128)}) custom-call(bf16[128,256]{1,0:T(8,128)(2,1)} %tokens_hbm.1, s32[2,128]{1,0:T(2,128)} %bitcast.13, f32[2,128]{1,0:T(2,128)} %bitcast.14, s32[1,128]{1,0:T(1,128)} %bitcast.15, f32[1,4096]{1,0:T(1,128)} %bitcast.12, bf16[128,128]{1,0:T(8,128)(2,1)} %target_hbm.1, ...), custom_call_target="tpu_custom_call" | custom-call | tf_op jit(solution)/shard_map/pallas_call | solution.py:505
  59.2 0.0 copy-start
  59.2 2.4 %copy.14 = bf16[1,128,4096]{2,1,0:T(8,128)(2,1)} copy(bf16[1,128,4096]{2,1,0:T(8,128)(2,1)} %bitcast.8) | data formatting | bytes 2097152
  61.6 0.0 copy-done
  61.6 1.0 %copy.15 = f32[256,1024]{1,0:T(8,128)} copy(f32[256,1024]{1,0:T(8,128)S(1)} %copy-done) | data formatting | bytes 2097152
Async XLA Ops:
  59.2 2.4 %copy-start = (f32[256,1024]{1,0:T(8,128)S(1)}, f32[256,1024]{1,0:T(8,128)}, u32[]{:S(2)}) copy-start(f32[256,1024]{1,0:T(8,128)} %get-tuple-element.9) | copy-start | bytes 3145732

commit v4 on v3

--- a/solution.py
+++ b/solution.py
@@ -182,7 +182,7 @@
 
     def dispatch(name, source, landing, work, beside):
         name_x = name + "_x"
-        for step in reversed(range(groups)):
+        for step in range(groups):
             to_group(name, step, source, landing.at[own_first + me], True)
         landing[own_first + me] = source[me]
 
@@ -388,7 +388,7 @@
     key_value = key_value + jnp.sum(proj_in[...].astype(f32), axis=0)
     cot[me] = (mask_ref[...].astype(f32) * (key_value - target) * token_rows ** (-0.5)).astype(bf16)
 
-    for step in reversed(range(1, groups)):
+    for step in range(1, groups):
         other = expert_at(swapped(me_group, step), me_mid, me_low)
         send("cot", step, cot.at[me], cot.at[me], (me_dp, other))
     for step in range(groups):

time: 62.7 us -> 61 us (0.973)
  Pallas kernels: 58.6 us -> 56.8 us
    pallas_call x1, Pallas kernels: 58.6 us -> 56.8 us  [per_device(): pl.pallas_call(functools.partial(kernel, dp_count, expert_count, top_coun...]
where the time goes in v4:
time: 61 us; the launch traced here: 60.8 us
  Pallas kernels  56.8 us (93%)
  local copies, waits for them, and re-layouts  3.35 us (5%)
  between operations  0.65 us (1%)
    pallas_call x1, Pallas kernels, per_device(): pl.pallas_call(functools.partial(kernel, dp_count, expert_count, top_coun...  56.8 us
    unnamed x4, local copies, waits for them, and re-layouts  3.35 us

profile of v4, /device:TPU:0, one launch (start us, length us, event | category | flops | bytes accessed | tf_op | source)
XLA Modules:
  0.0 60.8 jit_solution(13351846408691841519)
XLA Ops:
  0.6 56.8 %shard_map.113 = (bf16[128,4096]{1,0:T(8,128)(2,1)}, f32[256,1024]{1,0:T(8,128)}) custom-call(bf16[128,256]{1,0:T(8,128)(2,1)} %tokens_hbm.1, s32[2,128]{1,0:T(2,128)} %bitcast.13, f32[2,128]{1,0:T(2,128)} %bitcast.14, s32[1,128]{1,0:T(1,128)} %bitcast.15, f32[1,4096]{1,0:T(1,128)} %bitcast.12, bf16[128,128]{1,0:T(8,128)(2,1)} %target_hbm.1, ...), custom_call_target="tpu_custom_call" | custom-call | tf_op jit(solution)/shard_map/pallas_call | solution.py:505
  57.5 0.0 copy-start
  57.5 2.4 %copy.14 = bf16[1,128,4096]{2,1,0:T(8,128)(2,1)} copy(bf16[1,128,4096]{2,1,0:T(8,128)(2,1)} %bitcast.8) | data formatting | bytes 2097152
  59.9 0.0 copy-done
  59.9 1.0 %copy.15 = f32[256,1024]{1,0:T(8,128)} copy(f32[256,1024]{1,0:T(8,128)S(1)} %copy-done) | data formatting | bytes 2097152
Async XLA Ops:
  57.5 2.4 %copy-start = (f32[256,1024]{1,0:T(8,128)S(1)}, f32[256,1024]{1,0:T(8,128)}, u32[]{:S(2)}) copy-start(f32[256,1024]{1,0:T(8,128)} %get-tuple-element.9) | copy-start | bytes 3145732

commit v5 on v4

--- a/solution.py
+++ b/solution.py
@@ -265,7 +265,21 @@
             weights.append(jnp.concatenate([gate[span, :], up[span, :]], axis=1))
         sums[0] = sums[0] + dot(jnp.concatenate(sides, axis=1), jnp.concatenate(weights, axis=0), (1, 0))
 
-    dispatch("rows", rows_out, rows_in, up_projections, lambda step: None)
+    target_t = []
+    own_keys = kvw.shape[1] // expert_count
+
+    def beside_rows(step):
+        if step == 0:
+            loads[6].wait()
+            turned = kvw[...].T
+            for g in range(groups):
+                for mid in range(2):
+                    for low in range(2):
+                        c = expert_at(g, mid, low)
+                        kvw_t[low, mid, g] = turned[c * own_keys : (c + 1) * own_keys]
+            target_t.append(target_ref[...].astype(f32).T)
+
+    dispatch("rows", rows_out, rows_in, up_projections, beside_rows)
 
     row_number = lax.broadcasted_iota(jnp.int32, (rows, 1), 0)
     for b in range(dp_count):
@@ -315,16 +329,6 @@
 
     gather, prob_column = column_work()
     hidden_t = hidden_ref[...].astype(f32).T.astype(bf16)
-    loads[6].wait()
-    own_keys = kvw.shape[1] // expert_count
-    turned = kvw[...].T
-    for g in range(groups):
-        for mid in range(2):
-            for low in range(2):
-                c = expert_at(g, mid, low)
-                kvw_t[low, mid, g] = turned[c * own_keys : (c + 1) * own_keys]
-    target = target_ref[...].astype(f32).T
-
     for step in reversed(range(groups)):
         group = swapped(me_group, step)
         total = part_out[pl.ds(own_first + group * 4, 4)].astype(f32)
@@ -386,7 +390,7 @@
     leaves("proj", proj_in.at[pl.ds(0, groups - 1)])
     arrived("proj", 0, proj_in.at[pl.ds(0, groups - 1)])
     key_value = key_value + jnp.sum(proj_in[...].astype(f32), axis=0)
-    cot[me] = (mask_ref[...].astype(f32) * (key_value - target) * token_rows ** (-0.5)).astype(bf16)
+    cot[me] = (mask_ref[...].astype(f32) * (key_value - target_t[0]) * token_rows ** (-0.5)).astype(bf16)
 
     for step in range(1, groups):
         other = expert_at(swapped(me_group, step), me_mid, me_low)

time: 61 us -> 61 us (level)
  no operation moved by 1% of the time
where the time goes in v5:
time: 61 us; the launch traced here: 60.8 us
  Pallas kernels  56.8 us (93%)
  local copies, waits for them, and re-layouts  3.35 us (5%)
  between operations  0.65 us (1%)
    pallas_call x1, Pallas kernels, per_device(): pl.pallas_call(functools.partial(kernel, dp_count, expert_count, top_coun...  56.8 us
    unnamed x4, local copies, waits for them, and re-layouts  3.35 us

profile of v5, /device:TPU:0, one launch (start us, length us, event | category | flops | bytes accessed | tf_op | source)
XLA Modules:
  0.0 60.8 jit_solution(6583683931674182272)
XLA Ops:
  0.6 56.8 %shard_map.113 = (bf16[128,4096]{1,0:T(8,128)(2,1)}, f32[256,1024]{1,0:T(8,128)}) custom-call(bf16[128,256]{1,0:T(8,128)(2,1)} %tokens_hbm.1, s32[2,128]{1,0:T(2,128)} %bitcast.13, f32[2,128]{1,0:T(2,128)} %bitcast.14, s32[1,128]{1,0:T(1,128)} %bitcast.15, f32[1,4096]{1,0:T(1,128)} %bitcast.12, bf16[128,128]{1,0:T(8,128)(2,1)} %target_hbm.1, ...), custom_call_target="tpu_custom_call" | custom-call | tf_op jit(solution)/shard_map/pallas_call | solution.py:509
  57.5 0.0 copy-start
  57.5 2.4 %copy.14 = bf16[1,128,4096]{2,1,0:T(8,128)(2,1)} copy(bf16[1,128,4096]{2,1,0:T(8,128)(2,1)} %bitcast.8) | data formatting | bytes 2097152
  59.9 0.0 copy-done
  59.9 1.0 %copy.15 = f32[256,1024]{1,0:T(8,128)} copy(f32[256,1024]{1,0:T(8,128)S(1)} %copy-done) | data formatting | bytes 2097152
Async XLA Ops:
  57.5 2.4 %copy-start = (f32[256,1024]{1,0:T(8,128)S(1)}, f32[256,1024]{1,0:T(8,128)}, u32[]{:S(2)}) copy-start(f32[256,1024]{1,0:T(8,128)} %get-tuple-element.9) | copy-start | bytes 3145732
